TPU v7x, 128 devices: a whole 4x4x4 slice. The times are simulated.
128 devices in a mesh: tok: 8 (over z, y_hi), lat: 8 (over x, y_lo), src: 2 (over core).
Axes of the slice: x: 4, y: 4 (y_hi: 2, y_lo: 2; y = y_hi * 2 + y_lo), z: 4, core: 2. Of those that a mesh axis runs over, the one named last changes fastest.
Arguments:
- residuals: bfloat16 [2, 2048, 8192], P('src', 'tok', 'lat'), may hold values from -6 to 6
- enc_weight: bfloat16 [2, 8192, 16384], P('src', 'tok', 'lat'), may hold values from -0.046875 to 0.046875
- dec_weight: bfloat16 [2, 16384, 8192], P('src', 'lat', 'tok'), may hold values from -0.0625 to 0.0625
- enc_bias: float32 [16384], P('lat'), may hold values from -3 to 3
- dec_bias: float32 [2, 8192], P('src', 'tok'), may hold values from -3 to 3
- active: int32 [2048, 16384], P('tok', 'lat'), may hold values 0 or 1
Outputs:
- latent_codes: bfloat16 [2048, 16384], P('tok', 'lat')
- rebuilt: bfloat16 [2, 2048, 8192], P('src', 'lat', 'tok')
Inputs may be any that keep to these rules, and one draw needn't show every extreme that they name: `active`: each entry is 0 or 1. The number of kept latents of a token, or of a device's block, has no bound below the full shape that may be relied on.
All inputs are finite; a program needn't handle non-finite values.
Results may differ from a plain program's by a relative error of at most 0.0045.
Values may be sent and summed in bfloat16 or wider, within the bound.
A program may use at most 128 MiB of HBM per device.

v0:
```python
import jax
import jax.numpy as jnp
from jax import lax
from jax.sharding import PartitionSpec as P


def activate(pre_sum, enc_bias, chosen):
    positive = jnp.maximum(pre_sum + enc_bias[None, :], 0.0)
    return jnp.where(chosen == 1, positive, 0.0).astype(jnp.bfloat16)


def per_device(residuals, enc_weight, dec_weight, enc_bias, dec_bias, active):
    local_rows = residuals[0]
    relaid = lax.all_to_all(
        lax.all_to_all(local_rows, "lat", split_axis=0, concat_axis=1, tiled=True),
        "tok",
        split_axis=1,
        concat_axis=0,
        tiled=True,
    )
    tok_count = lax.axis_size("tok")
    grouped = relaid.reshape(tok_count, relaid.shape[0] // tok_count, relaid.shape[1])
    encoder = enc_weight[0]
    partial_value = jnp.einsum(
        "abd,dl->abl",
        lax.all_gather(grouped, "lat", axis=1, tiled=True),
        encoder,
        preferred_element_type=jnp.float32,
    )
    partial_value = partial_value.reshape(
        partial_value.shape[0] * partial_value.shape[1], partial_value.shape[2]
    )
    section_part = lax.psum_scatter(partial_value, "tok", scatter_dimension=0, tiled=True)
    both_sections = lax.psum(section_part, "src")
    own_rows = activate(both_sections, enc_bias, active)
    gathered = lax.all_gather(own_rows, "tok", axis=0, tiled=True)
    decoder = dec_weight[0]
    summed = lax.psum_scatter(
        jnp.dot(gathered, decoder, preferred_element_type=jnp.float32),
        "lat",
        scatter_dimension=0,
        tiled=True,
    )
    rebuilt = (summed + dec_bias[0][None, :]).astype(jnp.bfloat16)
    return (own_rows, rebuilt[None])


def solution(mesh):
    return jax.shard_map(
        per_device,
        mesh=mesh,
        in_specs=(
            P("src", "tok", "lat"),
            P("src", "tok", "lat"),
            P("src", "lat", "tok"),
            P("lat"),
            P("src", "tok"),
            P("tok", "lat"),
        ),
        out_specs=(P("tok", "lat"), P("src", "lat", "tok")),
        check_vma=False,
    )
```

profile of v0, /device:TPU:0, one launch (start us, length us, event | category | flops | bytes accessed | tf_op | source)
XLA Modules:
  0.0 667.3 jit_solution(14993558485904634929)
XLA Ops:
  7.2 0.0 all-gather.3.cloned.1.call-start
  7.2 15.1 %all_to_all.29 = bf16[8,32,1024]{2,1,0:T(8,128)(2,1)S(1)} all-to-all(bf16[8,32,1024]{2,1,0:T(8,128)(2,1)} %bitcast.17), channel_id=1, replica_groups=mesh['tok'=8,'lat'=8,'src'=2] {'lat'}, dimensions={0} | all-to-all | bytes 1048576 | tf_op jit(solution)/shard_map/all_to_all | solution.py:15
  22.3 17.7 %all_to_all.30 = bf16[32,8,1024]{2,0,1:T(8,128)(2,1)} all-to-all(bf16[32,8,1024]{2,0,1:T(8,128)(2,1)S(1)} %bitcast.16), channel_id=1, replica_groups=mesh['tok'=8,'lat'=8,'src'=2] {'tok'}, dimensions={1} | all-to-all | bytes 1048576 | tf_op jit(solution)/shard_map/all_to_all | solution.py:14
  40.1 0.0 all-gather.3.cloned.1.call-update
  40.1 0.0 reduce-scatter.3.cloned.1.call-start
  40.2 85.5 %all-gather.3.cloned.1.call-done = bf16[8,256,1024]{2,1,0:T(8,128)(2,1)} async-done(((bf16[8,32,1024]{2,1,0:T(8,128)(2,1)}), bf16[8,256,1024]{2,1,0:T(8,128)(2,1)}) %all-gather.3.cloned.1.call-update) | async-done | bytes 4194320 | tf_op jit(solution)/shard_map/all_gather | solution.py:26
  125.6 15.1 %fusion.2 = f32[2048,2048]{1,0:T(8,128)} fusion(bf16[2048,1024]{1,0:T(8,128)(2,1)} %bitcast.19, bf16[1,1024,2048]{2,1,0:T(8,128)(2,1)} %param.7), kind=kOutput, calls=%fused_computation.2 | convolution fusion | flops 8589934592 | bytes 25165824 | tf_op jit(solution)/shard_map/abd,dl->abl/dot_general | solution.py:24
  140.7 0.0 copy-start
  140.7 0.0 copy-start.1
  140.7 0.0 reduce-scatter.3.cloned.1.call-update
  140.8 0.0 all-reduce.2.cloned.1.call-start
  140.8 195.5 %reduce-scatter.3.cloned.1.call-done = f32[256,2048]{1,0:T(8,128)} async-done(((f32[2048,2048]{1,0:T(8,128)}), f32[256,2048]{1,0:T(8,128)}) %reduce-scatter.3.cloned.1.call-update) | async-done | bytes 2097168 | tf_op jit(solution)/shard_map/reduce_scatter | solution.py:33
  336.3 0.0 all-reduce.2.cloned.1.call-update
  336.3 0.0 all-gather.5.cloned.1.call-start
  336.3 29.0 %all-reduce.2.cloned.1.call-done = f32[256,2048]{1,0:T(8,128)} async-done(((f32[256,2048]{1,0:T(8,128)}), f32[256,2048]{1,0:T(8,128)}) %all-reduce.2.cloned.1.call-update) | async-done | bytes 2097168 | tf_op jit(solution)/shard_map/psum | solution.py:34
  365.4 0.0 copy-done
  365.4 0.0 copy-done.1
  365.4 3.0 select_convert_fusion
  368.3 0.0 all-gather.5.cloned.1.call-update
  368.4 0.0 reduce-scatter.5.cloned.1.call-start
  368.4 108.7 %all-gather.5.cloned.1.call-done = bf16[2048,2048]{1,0:T(8,128)(2,1)} async-done(((bf16[256,2048]{1,0:T(8,128)(2,1)}), bf16[2048,2048]{1,0:T(8,128)(2,1)}) %all-gather.5.cloned.1.call-update) | async-done | bytes 8388624 | tf_op jit(solution)/shard_map/all_gather | solution.py:36
  477.2 14.4 %fusion = f32[2048,1024]{1,0:T(8,128)} fusion(bf16[2048,2048]{1,0:T(8,128)(2,1)} %all-gather.5.cloned.1.call-done, bf16[1,2048,1024]{2,1,0:T(8,128)(2,1)} %param.8), kind=kOutput, calls=%fused_computation | convolution fusion | flops 8589934592 | bytes 20971520 | tf_op jit(solution)/shard_map/dot_general | solution.py:39
  491.6 0.0 copy-start.2
  491.6 0.0 reduce-scatter.5.cloned.1.call-update
  491.6 167.0 %reduce-scatter.5.cloned.1.call-done = f32[256,1024]{1,0:T(8,128)} async-done(((f32[2048,1024]{1,0:T(8,128)}), f32[256,1024]{1,0:T(8,128)}) %reduce-scatter.5.cloned.1.call-update) | async-done | bytes 1048592 | tf_op jit(solution)/shard_map/reduce_scatter | solution.py:38
  658.6 0.0 copy-done.2
  658.6 2.1 fusion.4
Async XLA Ops:
  7.2 118.5 %all-gather.3.cloned.1.call-start = ((), (), s32[]{:S(2)}) async-start(), calls=%async_computation.4 | async-start | bytes 4718592 | tf_op jit(solution)/shard_map/all_gather | solution.py:26
  40.1 296.2 %reduce-scatter.3.cloned.1.call-start = ((), (), s32[]{:S(2)}) async-start(), calls=%async_computation.5 | async-start | bytes 18874368 | tf_op jit(solution)/shard_map/reduce_scatter | solution.py:33
  140.7 224.6 %copy-start = (s32[256,2048]{1,0:T(8,128)S(1)}, s32[256,2048]{1,0:T(8,128)}, u32[]{:S(2)}) copy-start(s32[256,2048]{1,0:T(8,128)} %param.11) | copy-start | bytes 6291460
  140.7 224.6 %copy-start.1 = (f32[2048]{0:T(1024)S(1)}, f32[2048]{0:T(1024)}, u32[]{:S(2)}) copy-start(f32[2048]{0:T(1024)} %param.9) | copy-start | bytes 24580
  140.8 224.6 %all-reduce.2.cloned.1.call-start = ((), (), s32[]{:S(2)}) async-start(), calls=%async_computation.6 | async-start | bytes 4194304 | tf_op jit(solution)/shard_map/psum | solution.py:34
  336.3 140.9 %all-gather.5.cloned.1.call-start = ((), (), s32[]{:S(2)}) async-start(), calls=%async_computation.7 | async-start | bytes 9437184 | tf_op jit(solution)/shard_map/all_gather | solution.py:36
  368.4 290.3 %reduce-scatter.5.cloned.1.call-start = ((), (), s32[]{:S(2)}) async-start(), calls=%async_computation.8 | async-start | bytes 9437184 | tf_op jit(solution)/shard_map/reduce_scatter | solution.py:38
  491.6 167.1 %copy-start.2 = (f32[1,1024]{1,0:T(1,128)S(1)}, f32[1,1024]{1,0:T(1,128)}, u32[]{:S(2)}) copy-start(f32[1,1024]{1,0:T(1,128)} %param.10) | copy-start | bytes 12292
Sparse Core Ops, SparseCore 0:
  40.2 85.3 all-gather.2
  140.9 195.3 reduce-scatter.2
  338.9 26.4 all-reduce.1
  368.5 108.6 all-gather.4
  491.7 166.8 reduce-scatter.4
where the time goes:
time: 668 us; the launch traced here: 667 us
  waiting for transfers between devices  586 us (88%)
  blocking collectives  32.9 us (5%)
  matrix products  29.5 us (4%)
  between operations  13.8 us (2%)
    reduce_scatter x1, waiting for transfers between devices, per_device(): lax.psum_scatter(partial_value, 'tok', scatter_dimension=0, tiled=True)  195 us
    reduce_scatter x1, waiting for transfers between devices, per_device(): lax.psum_scatter(jnp.dot(gathered, decoder, preferred_element_type=jnp.fl...  167 us
    all_gather x1, waiting for transfers between devices, per_device(): gathered = lax.all_gather(own_rows, 'tok', axis=0, tiled=True)  109 us
    all_gather x1, waiting for transfers between devices, per_device(): lax.all_gather(grouped, 'lat', axis=1, tiled=True)  85.5 us
    psum x1, waiting for transfers between devices, per_device(): both_sections = lax.psum(section_part, 'src')  29 us
    all_to_all x1, blocking collectives, per_device(): lax.all_to_all(lax.all_to_all(local_rows, 'lat', split_axis=0, concat_axi...  17.7 us
    all_to_all x1, blocking collectives, per_device(): lax.all_to_all(local_rows, 'lat', split_axis=0, concat_axis=1, tiled=True)  15.1 us
    dot_general x1, matrix products, per_device(): jnp.einsum('abd,dl->abl', lax.all_gather(grouped, 'lat', axis=1, tiled=Tr...  15.1 us
  transfers between devices with their start and end apart: 5, of which 5 were waited for; matrix products, arithmetic and copies ran while one was open for 0% of the time, Pallas kernels for 0%

commit v1 on v0

v1 whole, which is shorter than its diff:
```python
import jax
import jax.numpy as jnp
from jax import lax
from jax.experimental import pallas as pl
from jax.experimental.pallas import tpu as pltpu
from jax.sharding import PartitionSpec as P

PARTS = 8
RING = 4
BF16 = jnp.bfloat16
F32 = jnp.float32


class Group:
    def __init__(self, axis):
        self.axis = axis
        self.me = lax.axis_index(axis)
        self.ring = self.me // 2
        self.half = self.me % 2
        self.right = self.at(1, self.half)
        self.left = self.at(3, self.half)
        self.partner = self.at(0, 1 - self.half)

    def at(self, step, half):
        return 2 * ((self.ring + step) % RING) + half

    def neighbours(self):
        return [{self.axis: self.right}, {self.axis: self.left}, {self.axis: self.partner}]


class Gather:
    def __init__(self, group, buf, send, recv, sub):
        self.group, self.buf, self.send, self.recv, self.sub = group, buf, send, recv, sub

    def copy(self, q, block, message, to):
        rows = pl.ds(pl.multiple_of(block * self.sub, self.sub), self.sub)
        place = self.buf.at[q, rows, :]
        return pltpu.make_async_remote_copy(
            place, place, self.send.at[q, message], self.recv.at[q, message],
            device_id={self.group.axis: to},
        )

    def first(self, q):
        g = self.group
        self.copy(q, g.me, 1, g.right).start()
        self.copy(q, g.me, 2, g.left).start()
        self.copy(q, g.me, 0, g.partner).start()

    def second(self, q):
        g = self.group
        self.copy(q, g.left, 1, g.right).wait_recv()
        self.copy(q, g.left, 5, g.right).start()
        self.copy(q, g.partner, 0, g.partner).wait_recv()
        self.copy(q, g.partner, 4, g.left).start()
        self.copy(q, g.partner, 3, g.right).start()
        self.copy(q, g.right, 2, g.right).wait_recv()

    def third(self, q):
        g = self.group
        self.copy(q, g.at(1, 1 - g.half), 4, g.right).wait_recv()
        self.copy(q, g.at(1, 1 - g.half), 6, g.left).start()
        self.copy(q, g.at(3, 1 - g.half), 3, g.right).wait_recv()

    def last(self, q):
        g = self.group
        self.copy(q, g.at(2, g.half), 5, g.right).wait_recv()
        self.copy(q, g.at(2, 1 - g.half), 6, g.right).wait_recv()

    def drain(self, q):
        g = self.group
        for message in range(7):
            self.copy(q, g.me, message, g.right).wait_send()


class Scatter:
    def __init__(self, group, sums, place, out1, in1, out2, in2, out3, in3, keep, send, recv, sub):
        self.group, self.sums, self.place = group, sums, place
        self.out1, self.in1, self.out2, self.in2 = out1, in1, out2, in2
        self.out3, self.in3, self.keep = out3, in3, keep
        self.send, self.recv, self.sub = send, recv, sub

    def rows(self, q, owner):
        start = pl.multiple_of(self.place(q, owner) * self.sub, self.sub)
        return self.sums[q % 4, pl.ds(start, self.sub), :]

    def copy(self, q, message):
        g = self.group
        src, dst = {
            0: (self.out1.at[q, 0], self.in1.at[q, 0]),
            1: (self.out1.at[q, 1], self.in1.at[q, 1]),
            2: (self.out2.at[q, 0], self.in2.at[q, 0]),
            3: (self.out2.at[q, 1], self.in2.at[q, 1]),
            4: (self.out3.at[q], self.in3.at[q]),
        }[message]
        to = g.partner if message == 4 else (g.right, g.left)[message % 2]
        return pltpu.make_async_remote_copy(
            src, dst, self.send.at[q, message], self.recv.at[q, message], device_id={g.axis: to}
        )

    def first(self, q):
        for h in (0, 1):
            self.out1[q, h] = self.rows(q, self.group.at(2, h)).astype(BF16)
            self.copy(q, h).start()

    def second(self, q):
        g, sub = self.group, self.sub
        for side, step in ((0, 1), (1, 3)):
            self.copy(q, side).wait_recv()
            for h in (0, 1):
                value = self.rows(q, g.at(step, h))
                if h == side:
                    value = value + self.in1[q, side].astype(F32)
                self.out2[q, side, h * sub:(h + 1) * sub, :] = value.astype(BF16)
            self.copy(q, 2 + side).start()

    def third(self, q):
        g, sub = self.group, self.sub
        self.copy(q, 2).wait_recv()
        self.copy(q, 3).wait_recv()

        def total(h):
            rows = pl.ds(pl.multiple_of(h * sub, sub), sub)
            return (
                self.rows(q, g.at(0, h))
                + self.in2[q, 0, rows, :].astype(F32)
                + self.in2[q, 1, rows, :].astype(F32)
            )

        self.out3[q] = total(1 - g.half).astype(self.out3.dtype)
        self.copy(q, 4).start()
        self.keep[q] = total(g.half)

    def last(self, q):
        self.copy(q, 4).wait_recv()
        return self.keep[q] + self.in3[q].astype(F32)

    def drain(self, q):
        for message in range(5):
            self.copy(q, message).wait_send()


def product(a, a_other, w, w_other, sums, q, arrived):
    cols = sums.shape[2]
    tile = 256
    for part in range(cols // tile):
        at = slice(part * tile, (part + 1) * tile)
        sums[q % 4, :, at] = jnp.dot(a[q], w[:, at], preferred_element_type=F32)
    arrived()
    for part in range(cols // tile):
        at = slice(part * tile, (part + 1) * tile)
        sums[q % 4, :, at] += jnp.dot(a_other[q], w_other[:, at], preferred_element_type=F32)


def kernel(
    res, encw, decw, encb, decb, active,
    codes_out, rebuilt_out,
    x_own, x_sib, c_own, c_sib, we_own, we_sib, wd_own, wd_sib, mask, made,
    e_sums, e_out1, e_in1, e_out2, e_in2, e_out3, e_in3, e_keep,
    d_sums, d_out1, d_in1, d_out2, d_in2, d_out3, d_in3, d_keep,
    a2a_send, a2a_recv, local_sem, wx_sem,
    xg_send, xg_recv, cg_send, cg_recv,
    xs_send, xs_recv, cs_send, cs_recv,
    er_send, er_recv, dr_send, dr_recv, co_sem, ro_sem,
):
    tok, lat, core = Group("tok"), Group("lat"), lax.axis_index("src")
    t, l = tok.me, lat.me
    sibling = {"src": 1 - core}
    width = x_own.shape[2]
    sub = x_own.shape[1] // PARTS
    alone = t == l

    def half(which):
        return pl.ds(pl.multiple_of(which * width, width), width)

    def block(index):
        return pl.ds(pl.multiple_of(index * sub, sub), sub)

    loads = [
        pltpu.make_async_copy(encw.at[:, half(core)], we_own, local_sem.at[0]),
        pltpu.make_async_copy(decw.at[half(core), :], wd_own, local_sem.at[1]),
        pltpu.make_async_copy(decw.at[half(1 - core), :], wd_sib, local_sem.at[2]),
        pltpu.make_async_copy(active.at[:, half(core)], mask, local_sem.at[3]),
    ]
    for load in loads:
        load.start()

    barrier = pltpu.get_barrier_semaphore()
    for device in tok.neighbours() + lat.neighbours() + [sibling]:
        pl.semaphore_signal(barrier, inc=1, device_id=device)

    @pl.loop(0, PARTS)
    def _(i):
        @pl.when(jnp.logical_not(alone & (i == t)))
        def _():
            pl.semaphore_signal(barrier, inc=1, device_id={"tok": i, "lat": t})

    pl.semaphore_wait(barrier, jnp.where(alone, 14, 15))

    def relay(q):
        j = (t - q + PARTS) % PARTS
        return pltpu.make_async_remote_copy(
            res.at[block(j), :], x_own.at[q, block(j), :], a2a_send.at[q], a2a_recv.at[q],
            device_id={"tok": l, "lat": j},
        )

    def stay():
        return pltpu.make_async_copy(res.at[block(l), :], x_own.at[0, block(l), :], a2a_recv.at[0])

    @pl.loop(0, PARTS)
    def _(q):
        own = alone & (q == 0)

        @pl.when(own)
        def _():
            stay().start()

        @pl.when(jnp.logical_not(own))
        def _():
            relay(q).start()

    def landed(q):
        own = alone & (q == 0)
        place = x_own.at[q, block(l), :]

        @pl.when(own)
        def _():
            stay().wait()

        @pl.when(jnp.logical_not(own))
        def _():
            pltpu.make_async_remote_copy(
                place, place, a2a_send.at[q], a2a_recv.at[q], device_id=sibling
            ).wait_recv()

    swap = pltpu.make_async_remote_copy(
        encw.at[:, half(1 - core)], we_sib, wx_sem.at[0], wx_sem.at[1], device_id=sibling
    )
    swap.start()

    xg = Gather(lat, x_own, xg_send, xg_recv, sub)
    cg = Gather(tok, c_own, cg_send, cg_recv, sub)
    er = Scatter(
        tok, e_sums, lambda q, owner: (owner - q + PARTS) % PARTS,
        e_out1, e_in1, e_out2, e_in2, e_out3, e_in3, e_keep, er_send, er_recv, sub,
    )
    dr = Scatter(
        lat, d_sums, lambda q, owner: owner,
        d_out1, d_in1, d_out2, d_in2, d_out3, d_in3, d_keep, dr_send, dr_recv, sub,
    )

    def x_swap(q):
        return pltpu.make_async_remote_copy(
            x_own.at[q], x_sib.at[q], xs_send.at[q], xs_recv.at[q], device_id=sibling
        )

    def c_swap(q):
        return pltpu.make_async_remote_copy(
            c_own.at[q], c_sib.at[q], cs_send.at[q], cs_recv.at[q], device_id=sibling
        )

    def codes_copy(q, which):
        rows = block((t - q + PARTS) % PARTS)
        src = c_sib if which else c_own
        col = (1 - core) if which else core
        return pltpu.make_async_copy(
            src.at[q, block(t), :], codes_out.at[rows, half(col)], co_sem.at[q, which]
        )

    def rebuilt_copy(q):
        rows = block((l - q + PARTS) % PARTS)
        return pltpu.make_async_copy(made.at[q], rebuilt_out.at[rows, :], ro_sem.at[q])

    def s0(q):
        landed(q)
        xg.first(q)

    def s3(q):
        xg.last(q)
        x_swap(q).start()

        @pl.when(q == 0)
        def _():
            loads[0].wait()
            swap.wait()

        product(x_own, x_sib, we_own, we_sib, e_sums, q, lambda: x_swap(q).wait_recv())
        er.first(q)

    def s6(q):
        @pl.when(q == 0)
        def _():
            loads[3].wait()

        value = er.last(q) + encb[pl.ds(core, 1), :]
        kept = mask[block((t - q + PARTS) % PARTS), :] == 1
        c_own[q, block(t), :] = jnp.where(kept, jnp.maximum(value, 0.0), 0.0).astype(BF16)
        cg.first(q)
        codes_copy(q, 0).start()

    def s9(q):
        cg.last(q)
        c_swap(q).start()

        @pl.when(q == 0)
        def _():
            loads[1].wait()
            loads[2].wait()

        product(c_own, c_sib, wd_own, wd_sib, d_sums, q, lambda: c_swap(q).wait_recv())
        dr.first(q)
        codes_copy(q, 1).start()

    def s12(q):
        made[q] = (dr.last(q) + decb[...]).astype(BF16)
        rebuilt_copy(q).start()

    stages = [
        s0, xg.second, xg.third, s3, er.second, er.third, s6,
        cg.second, cg.third, s9, dr.second, dr.third, s12,
    ]

    @pl.loop(0, PARTS + len(stages) - 1)
    def _(i):
        for number, stage in reversed(list(enumerate(stages))):
            q = i - number

            @pl.when((q >= 0) & (q < PARTS))
            def _(stage=stage, q=q):
                stage(q)

    @pl.loop(0, PARTS)
    def _(q):
        @pl.when(jnp.logical_not(alone & (q == 0)))
        def _():
            relay(q).wait_send()

        xg.drain(q)
        cg.drain(q)
        er.drain(q)
        dr.drain(q)
        x_swap(q).wait_send()
        c_swap(q).wait_send()
        codes_copy(q, 0).wait()
        codes_copy(q, 1).wait()
        rebuilt_copy(q).wait()


def per_device(residuals, enc_weight, dec_weight, enc_bias, dec_bias, active):
    rows, width = residuals.shape[1:]
    latents = enc_weight.shape[2]
    sub = rows // PARTS
    dma = pltpu.SemaphoreType.DMA

    def reduction():
        return [
            pltpu.VMEM((4, rows, width), F32),
            pltpu.VMEM((PARTS, 2, sub, width), BF16),
            pltpu.VMEM((PARTS, 2, sub, width), BF16),
            pltpu.VMEM((PARTS, 2, 2 * sub, width), BF16),
            pltpu.VMEM((PARTS, 2, 2 * sub, width), BF16),
            pltpu.VMEM((PARTS, sub, width), BF16),
            pltpu.VMEM((PARTS, sub, width), BF16),
            pltpu.VMEM((PARTS, sub, width), F32),
        ]

    anywhere = pl.BlockSpec(memory_space=pl.ANY)
    vmem = pl.BlockSpec(memory_space=pltpu.VMEM)
    codes, rebuilt = pl.pallas_call(
        kernel,
        out_shape=(
            jax.ShapeDtypeStruct((rows, latents), BF16),
            jax.ShapeDtypeStruct((rows, width), BF16),
        ),
        in_specs=[anywhere, anywhere, anywhere, vmem, vmem, anywhere],
        out_specs=(anywhere, anywhere),
        scratch_shapes=[pltpu.VMEM((PARTS, rows, width), BF16)] * 4
        + [pltpu.VMEM((width, width), BF16)] * 4
        + [pltpu.VMEM((rows, width), jnp.int32), pltpu.VMEM((PARTS, sub, width), BF16)]
        + reduction()
        + reduction()
        + [dma((PARTS,)), dma((PARTS,)), dma((4,)), dma((2,))]
        + [dma((PARTS, 7))] * 4
        + [dma((PARTS,))] * 4
        + [dma((PARTS, 5))] * 4
        + [dma((PARTS, 2)), dma((PARTS,))],
        compiler_params=pltpu.CompilerParams(
            collective_id=0, has_side_effects=True, vmem_limit_bytes=60 * 1024 * 1024
        ),
    )(
        residuals[0], enc_weight[0], dec_weight[0],
        enc_bias.reshape(2, width), dec_bias, active,
    )
    return codes, rebuilt[None]


def solution(mesh):
    return jax.shard_map(
        per_device,
        mesh=mesh,
        in_specs=(
            P("src", "tok", "lat"),
            P("src", "tok", "lat"),
            P("src", "lat", "tok"),
            P("lat"),
            P("src", "tok"),
            P("tok", "lat"),
        ),
        out_specs=(P("tok", "lat"), P("src", "lat", "tok")),
        check_vma=False,
    )
```

time: 668 us -> 140 us (0.21)
  waiting for transfers between devices: 586 us -> 0 us
  Pallas kernels: 0 us -> 134 us
  blocking collectives: 32.9 us -> 0 us
  matrix products: 29.5 us -> 0 us
  between operations: 13.8 us -> 0.64 us
    reduce_scatter x2 -> x0, waiting for transfers between devices: 363 us -> none  [the longest x1 195 us: per_device(): lax.psum_scatter(partial_value, 'tok', scatter_dimension=0, tiled=True)]
    all_gather x2 -> x0, waiting for transfers between devices: 194 us -> none  [the longest x1 109 us: per_device(): gathered = lax.all_gather(own_rows, 'tok', axis=0, tiled=True)]
    pallas_call x0 -> x1, Pallas kernels: none -> 134 us  [per_device(): pl.pallas_call(kernel, out_shape=(jax.ShapeDtypeStruct((rows, latents), B...]
    all_to_all x2 -> x0, blocking collectives: 32.9 us -> none  [the longest x1 17.7 us: per_device(): lax.all_to_all(lax.all_to_all(local_rows, 'lat', split_axis=0, concat_axi...]
    dot_general x2 -> x0, matrix products: 29.5 us -> none  [the longest x1 15.1 us: per_device(): jnp.einsum('abd,dl->abl', lax.all_gather(grouped, 'lat', axis=1, tiled=Tr...]
    psum x1 -> x0, waiting for transfers between devices: 29 us -> none  [per_device(): both_sections = lax.psum(section_part, 'src')]
  transfers between devices with their start and end apart: 5 -> 0, of which waited for: 5 -> 0; matrix products, arithmetic and copies ran while one was open for 0% -> 0% of each run, Pallas kernels for 0% -> 0%
where the time goes in v1:
time: 140 us
  Pallas kernels  134 us (96%)
  local copies, waits for them, and re-layouts  5.48 us (4%)
    pallas_call x1, Pallas kernels, per_device(): pl.pallas_call(kernel, out_shape=(jax.ShapeDtypeStruct((rows, latents), B...  134 us
    unnamed x2, local copies, waits for them, and re-layouts  4.17 us

profile of v1, /device:TPU:0, one launch (start us, length us, event | category | flops | bytes accessed | tf_op | source)
XLA Modules:
  0.0 139.8 jit_solution(16336496073492343844)
XLA Ops:
  0.6 1.3 reshape.7.encb
  1.9 133.7 %shard_map.77 = (bf16[256,2048]{1,0:T(8,128)(2,1)}, bf16[256,1024]{1,0:T(8,128)(2,1)}) custom-call(bf16[256,1024]{1,0:T(8,128)(2,1)} %bitcast.6, bf16[1024,2048]{1,0:T(8,128)(2,1)} %bitcast.4, bf16[2048,1024]{1,0:T(8,128)(2,1)} %bitcast.5, f32[2,1024]{1,0:T(2,128)} %reshape.7.encb, f32[1,1024]{1,0:T(1,128)} %decb.1, s32[256,2048]{1,0:T(8,128)} %active.1), custom_call_target="tpu_custom_call" | custom-call | tf_op jit(solution)/shard_map/pallas_call | solution.py:368
  135.7 2.3 %copy.10 = bf16[256,2048]{1,0:T(8,128)(2,1)} copy(bf16[256,2048]{1,0:T(8,128)(2,1)} %get-tuple-element.8) | data formatting | bytes 2097152
  138.0 1.9 %copy.11 = bf16[1,256,1024]{2,1,0:T(8,128)(2,1)} copy(bf16[1,256,1024]{2,1,0:T(8,128)(2,1)} %bitcast.7) | data formatting | bytes 1048576

commit v2 on v1

--- a/solution.py
+++ b/solution.py
@@ -6,6 +6,7 @@
 from jax.sharding import PartitionSpec as P
 
 PARTS = 8
+SLOTS = 6
 RING = 4
 BF16 = jnp.bfloat16
 F32 = jnp.float32
@@ -36,7 +37,7 @@
         rows = pl.ds(pl.multiple_of(block * self.sub, self.sub), self.sub)
         place = self.buf.at[q, rows, :]
         return pltpu.make_async_remote_copy(
-            place, place, self.send.at[q, message], self.recv.at[q, message],
+            place, place, self.send.at[0], self.recv.at[q, (1, 0, 3, 3, 2, 3, 3)[message]],
             device_id={self.group.axis: to},
         )
 
@@ -46,30 +47,27 @@
         self.copy(q, g.me, 2, g.left).start()
         self.copy(q, g.me, 0, g.partner).start()
 
-    def second(self, q):
+    def pass_left(self, q):
         g = self.group
         self.copy(q, g.left, 1, g.right).wait_recv()
         self.copy(q, g.left, 5, g.right).start()
+
+    def pass_partner(self, q):
+        g = self.group
         self.copy(q, g.partner, 0, g.partner).wait_recv()
         self.copy(q, g.partner, 4, g.left).start()
         self.copy(q, g.partner, 3, g.right).start()
-        self.copy(q, g.right, 2, g.right).wait_recv()
-
-    def third(self, q):
+
+    def pass_corner(self, q):
         g = self.group
         self.copy(q, g.at(1, 1 - g.half), 4, g.right).wait_recv()
         self.copy(q, g.at(1, 1 - g.half), 6, g.left).start()
-        self.copy(q, g.at(3, 1 - g.half), 3, g.right).wait_recv()
 
     def last(self, q):
-        g = self.group
-        self.copy(q, g.at(2, g.half), 5, g.right).wait_recv()
-        self.copy(q, g.at(2, 1 - g.half), 6, g.right).wait_recv()
-
-    def drain(self, q):
-        g = self.group
-        for message in range(7):
-            self.copy(q, g.me, message, g.right).wait_send()
+        rest = self.buf.at[q, pl.ds(0, 4 * self.sub), :]
+        pltpu.make_async_remote_copy(
+            rest, rest, self.send.at[0], self.recv.at[q, 3], device_id={self.group.axis: self.group.right}
+        ).wait_recv()
 
 
 class Scatter:
@@ -81,7 +79,7 @@
 
     def rows(self, q, owner):
         start = pl.multiple_of(self.place(q, owner) * self.sub, self.sub)
-        return self.sums[q % 4, pl.ds(start, self.sub), :]
+        return self.sums[q % SLOTS, pl.ds(start, self.sub), :]
 
     def copy(self, q, message):
         g = self.group
@@ -94,7 +92,7 @@
         }[message]
         to = g.partner if message == 4 else (g.right, g.left)[message % 2]
         return pltpu.make_async_remote_copy(
-            src, dst, self.send.at[q, message], self.recv.at[q, message], device_id={g.axis: to}
+            src, dst, self.send.at[0], self.recv.at[q, (0, 1, 2, 2, 3)[message]], device_id={g.axis: to}
         )
 
     def first(self, q):
@@ -115,8 +113,9 @@
 
     def third(self, q):
         g, sub = self.group, self.sub
-        self.copy(q, 2).wait_recv()
-        self.copy(q, 3).wait_recv()
+        pltpu.make_async_remote_copy(
+            self.out2.at[q], self.in2.at[q], self.send.at[0], self.recv.at[q, 2], device_id={g.axis: g.right}
+        ).wait_recv()
 
         def total(h):
             rows = pl.ds(pl.multiple_of(h * sub, sub), sub)
@@ -134,21 +133,17 @@
         self.copy(q, 4).wait_recv()
         return self.keep[q] + self.in3[q].astype(F32)
 
-    def drain(self, q):
-        for message in range(5):
-            self.copy(q, message).wait_send()
-
 
 def product(a, a_other, w, w_other, sums, q, arrived):
     cols = sums.shape[2]
     tile = 256
     for part in range(cols // tile):
         at = slice(part * tile, (part + 1) * tile)
-        sums[q % 4, :, at] = jnp.dot(a[q], w[:, at], preferred_element_type=F32)
+        sums[q % SLOTS, :, at] = jnp.dot(a[q], w[:, at], preferred_element_type=F32)
     arrived()
     for part in range(cols // tile):
         at = slice(part * tile, (part + 1) * tile)
-        sums[q % 4, :, at] += jnp.dot(a_other[q], w_other[:, at], preferred_element_type=F32)
+        sums[q % SLOTS, :, at] += jnp.dot(a_other[q], w_other[:, at], preferred_element_type=F32)
 
 
 def kernel(
@@ -199,7 +194,7 @@
     def relay(q):
         j = (t - q + PARTS) % PARTS
         return pltpu.make_async_remote_copy(
-            res.at[block(j), :], x_own.at[q, block(j), :], a2a_send.at[q], a2a_recv.at[q],
+            res.at[block(j), :], x_own.at[q, block(j), :], a2a_send.at[0], a2a_recv.at[q],
             device_id={"tok": l, "lat": j},
         )
 
@@ -229,7 +224,7 @@
         @pl.when(jnp.logical_not(own))
         def _():
             pltpu.make_async_remote_copy(
-                place, place, a2a_send.at[q], a2a_recv.at[q], device_id=sibling
+                place, place, a2a_send.at[0], a2a_recv.at[q], device_id=sibling
             ).wait_recv()
 
     swap = pltpu.make_async_remote_copy(
@@ -250,12 +245,12 @@
 
     def x_swap(q):
         return pltpu.make_async_remote_copy(
-            x_own.at[q], x_sib.at[q], xs_send.at[q], xs_recv.at[q], device_id=sibling
+            x_own.at[q], x_sib.at[q], xs_send.at[0], xs_recv.at[q], device_id=sibling
         )
 
     def c_swap(q):
         return pltpu.make_async_remote_copy(
-            c_own.at[q], c_sib.at[q], cs_send.at[q], cs_recv.at[q], device_id=sibling
+            c_own.at[q], c_sib.at[q], cs_send.at[0], cs_recv.at[q], device_id=sibling
         )
 
     def codes_copy(q, which):
@@ -263,44 +258,46 @@
         src = c_sib if which else c_own
         col = (1 - core) if which else core
         return pltpu.make_async_copy(
-            src.at[q, block(t), :], codes_out.at[rows, half(col)], co_sem.at[q, which]
+            src.at[q, block(t), :], codes_out.at[rows, half(col)], co_sem.at[0]
         )
 
     def rebuilt_copy(q):
         rows = block((l - q + PARTS) % PARTS)
-        return pltpu.make_async_copy(made.at[q], rebuilt_out.at[rows, :], ro_sem.at[q])
-
-    def s0(q):
+        return pltpu.make_async_copy(made.at[q], rebuilt_out.at[rows, :], ro_sem.at[0])
+
+    def x_first(q):
         landed(q)
         xg.first(q)
 
-    def s3(q):
+    def x_last(q):
         xg.last(q)
         x_swap(q).start()
 
+    def encode(q):
         @pl.when(q == 0)
         def _():
             loads[0].wait()
-            swap.wait()
+            swap.wait_recv()
 
         product(x_own, x_sib, we_own, we_sib, e_sums, q, lambda: x_swap(q).wait_recv())
         er.first(q)
 
-    def s6(q):
+    def activate(q):
         @pl.when(q == 0)
         def _():
             loads[3].wait()
 
-        value = er.last(q) + encb[pl.ds(core, 1), :]
+        value = er.last(q) + encb[:, half(core)]
         kept = mask[block((t - q + PARTS) % PARTS), :] == 1
         c_own[q, block(t), :] = jnp.where(kept, jnp.maximum(value, 0.0), 0.0).astype(BF16)
         cg.first(q)
         codes_copy(q, 0).start()
 
-    def s9(q):
+    def c_last(q):
         cg.last(q)
         c_swap(q).start()
 
+    def decode(q):
         @pl.when(q == 0)
         def _():
             loads[1].wait()
@@ -310,39 +307,65 @@
         dr.first(q)
         codes_copy(q, 1).start()
 
-    def s12(q):
+    def finish(q):
         made[q] = (dr.last(q) + decb[...]).astype(BF16)
         rebuilt_copy(q).start()
 
-    stages = [
-        s0, xg.second, xg.third, s3, er.second, er.third, s6,
-        cg.second, cg.third, s9, dr.second, dr.third, s12,
+    steps = [
+        (encode, 5),
+        (dr.third, 17),
+        (dr.second, 13),
+        (cg.pass_corner, 10),
+        (cg.pass_partner, 9),
+        (er.second, 6),
+        (x_last, 4),
+        (xg.pass_corner, 3),
+        (xg.pass_left, 2),
+        (x_first, 0),
+        (xg.pass_partner, 1),
+        (activate, 8),
+        (er.third, 7),
+        (decode, 11),
+        (finish, 19),
+        (cg.pass_left, 9),
+        (c_last, 10),
     ]
-
-    @pl.loop(0, PARTS + len(stages) - 1)
+    rounds = PARTS + max(lag for _, lag in steps)
+
+    @pl.loop(0, rounds)
     def _(i):
-        for number, stage in reversed(list(enumerate(stages))):
-            q = i - number
+        for step, lag in steps:
+            q = i - lag
 
             @pl.when((q >= 0) & (q < PARTS))
-            def _(stage=stage, q=q):
-                stage(q)
-
-    @pl.loop(0, PARTS)
-    def _(q):
-        @pl.when(jnp.logical_not(alone & (q == 0)))
-        def _():
-            relay(q).wait_send()
-
-        xg.drain(q)
-        cg.drain(q)
-        er.drain(q)
-        dr.drain(q)
-        x_swap(q).wait_send()
-        c_swap(q).wait_send()
-        codes_copy(q, 0).wait()
-        codes_copy(q, 1).wait()
-        rebuilt_copy(q).wait()
+            def _(step=step, q=q):
+                step(q)
+
+    def sent(src, sem):
+        pltpu.make_async_remote_copy(src, src, sem, a2a_recv.at[0], device_id=sibling).wait_send()
+
+    most = pl.ds(0, PARTS - 1)
+    for sem in (xg_send, cg_send, er_send, dr_send):
+        sent(x_own.at[most], sem.at[0])
+    sent(x_own, xs_send.at[0])
+    sent(c_own, cs_send.at[0])
+    swap.wait_send()
+
+    @pl.when(alone)
+    def _():
+        sent(res.at[pl.ds(0, (PARTS - 1) * sub), :], a2a_send.at[0])
+
+    @pl.when(jnp.logical_not(alone))
+    def _():
+        sent(res, a2a_send.at[0])
+
+    pltpu.make_async_copy(codes_out, codes_out, co_sem.at[0]).wait()
+    pltpu.make_async_copy(rebuilt_out, rebuilt_out, ro_sem.at[0]).wait()
+
+
+def deliver(codes_in, rebuilt_in, codes_out, rebuilt_out):
+    codes_out[...] = codes_in[...]
+    rebuilt_out[...] = rebuilt_in[...]
 
 
 def per_device(residuals, enc_weight, dec_weight, enc_bias, dec_bias, active):
@@ -353,7 +376,7 @@
 
     def reduction():
         return [
-            pltpu.VMEM((4, rows, width), F32),
+            pltpu.VMEM((SLOTS, rows, width), F32),
             pltpu.VMEM((PARTS, 2, sub, width), BF16),
             pltpu.VMEM((PARTS, 2, sub, width), BF16),
             pltpu.VMEM((PARTS, 2, 2 * sub, width), BF16),
@@ -378,18 +401,28 @@
         + [pltpu.VMEM((rows, width), jnp.int32), pltpu.VMEM((PARTS, sub, width), BF16)]
         + reduction()
         + reduction()
-        + [dma((PARTS,)), dma((PARTS,)), dma((4,)), dma((2,))]
-        + [dma((PARTS, 7))] * 4
-        + [dma((PARTS,))] * 4
-        + [dma((PARTS, 5))] * 4
-        + [dma((PARTS, 2)), dma((PARTS,))],
+        + [dma((1,)), dma((PARTS,)), dma((4,)), dma((2,))]
+        + [dma((1,)), dma((PARTS, 4))] * 2
+        + [dma((1,)), dma((PARTS,))] * 2
+        + [dma((1,)), dma((PARTS, 4))] * 2
+        + [dma((1,)), dma((1,))],
         compiler_params=pltpu.CompilerParams(
             collective_id=0, has_side_effects=True, vmem_limit_bytes=60 * 1024 * 1024
         ),
     )(
         residuals[0], enc_weight[0], dec_weight[0],
-        enc_bias.reshape(2, width), dec_bias, active,
+        enc_bias.reshape(1, latents), dec_bias, active,
     )
+    codes, rebuilt = pl.pallas_call(
+        deliver,
+        out_shape=(
+            jax.ShapeDtypeStruct(codes.shape, BF16),
+            jax.ShapeDtypeStruct(rebuilt.shape, BF16),
+        ),
+        grid=(2,),
+        in_specs=[pl.BlockSpec((rows // 2, latents), lambda i: (i, 0)), pl.BlockSpec((rows // 2, width), lambda i: (i, 0))],
+        out_specs=(pl.BlockSpec((rows // 2, latents), lambda i: (i, 0)), pl.BlockSpec((rows // 2, width), lambda i: (i, 0))),
+    )(codes, rebuilt)
     return codes, rebuilt[None]
 
 

time: 140 us -> 128 us (0.914)
  Pallas kernels: 134 us -> 126 us
  local copies, waits for them, and re-layouts: 5.48 us -> 0 us
    pallas_call x1, Pallas kernels: 134 us -> 124 us  [per_device(): pl.pallas_call(kernel, out_shape=(jax.ShapeDtypeStruct((rows, latents), B...]
    unnamed x2 -> x0, local copies, waits for them, and re-layouts: 4.17 us -> none
    pallas_call x0 -> x1, Pallas kernels: none -> 2.31 us  [per_device(): pl.pallas_call(deliver, out_shape=(jax.ShapeDtypeStruct(codes.shape, BF16...]
where the time goes in v2:
time: 128 us; the launch traced here: 127 us
  Pallas kernels  126 us (98%)
    pallas_call x1, Pallas kernels, per_device(): pl.pallas_call(kernel, out_shape=(jax.ShapeDtypeStruct((rows, latents), B...  124 us

profile of v2, /device:TPU:0, one launch (start us, length us, event | category | flops | bytes accessed | tf_op | source)
XLA Modules:
  0.0 127.1 jit_solution(1038600585409542968)
XLA Ops:
  0.6 124.1 %shard_map.77 = (bf16[256,2048]{1,0:T(8,128)(2,1)}, bf16[256,1024]{1,0:T(8,128)(2,1)}) custom-call(bf16[256,1024]{1,0:T(8,128)(2,1)} %bitcast.7, bf16[1024,2048]{1,0:T(8,128)(2,1)} %bitcast.5, bf16[2048,1024]{1,0:T(8,128)(2,1)} %bitcast.6, f32[1,2048]{1,0:T(1,128)} %bitcast.8, f32[1,1024]{1,0:T(1,128)} %decb.1, s32[256,2048]{1,0:T(8,128)} %active.1), custom_call_target="tpu_custom_call" | custom-call | tf_op jit(solution)/shard_map/pallas_call | solution.py:391
  124.8 2.3 %shard_map.78 = (bf16[256,2048]{1,0:T(8,128)(2,1)}, bf16[256,1024]{1,0:T(8,128)(2,1)}) custom-call(bf16[256,2048]{1,0:T(8,128)(2,1)} %get-tuple-element.6.codes_in, bf16[256,1024]{1,0:T(8,128)(2,1)} %get-tuple-element.7.rebuilt_in), custom_call_target="tpu_custom_call" | custom-call | tf_op jit(solution)/shard_map/pallas_call | solution.py:416

commit v3 on v2

--- a/solution.py
+++ b/solution.py
@@ -7,6 +7,9 @@
 
 PARTS = 8
 SLOTS = 6
+PAIR_FIRST = (5, 6, 7)
+LAT_FIRST = ()
+PAIR_LAST = ()
 RING = 4
 BF16 = jnp.bfloat16
 F32 = jnp.float32
@@ -29,39 +32,87 @@
         return [{self.axis: self.right}, {self.axis: self.left}, {self.axis: self.partner}]
 
 
+def either(q, chunks, special, usual):
+    if not chunks:
+        usual(q)
+        return
+    named = q == chunks[0]
+    for chunk in chunks[1:]:
+        named = named | (q == chunk)
+
+    @pl.when(named)
+    def _():
+        special(q)
+
+    @pl.when(jnp.logical_not(named))
+    def _():
+        usual(q)
+
+
 class Gather:
-    def __init__(self, group, buf, send, recv, sub):
+    def __init__(self, group, buf, send, recv, sub, pair_last=()):
         self.group, self.buf, self.send, self.recv, self.sub = group, buf, send, recv, sub
-
-    def copy(self, q, block, message, to):
-        rows = pl.ds(pl.multiple_of(block * self.sub, self.sub), self.sub)
-        place = self.buf.at[q, rows, :]
+        self.pair_last = pair_last
+
+    def copy(self, q, block, sem, to, skip=0, rows=None):
+        rows = rows or self.sub
+        start = pl.multiple_of(block * self.sub + skip, rows)
+        place = self.buf.at[q, pl.ds(start, rows), :]
         return pltpu.make_async_remote_copy(
-            place, place, self.send.at[0], self.recv.at[q, (1, 0, 3, 3, 2, 3, 3)[message]],
-            device_id={self.group.axis: to},
+            place, place, self.send.at[0], self.recv.at[q, sem], device_id={self.group.axis: to}
         )
 
     def first(self, q):
         g = self.group
-        self.copy(q, g.me, 1, g.right).start()
-        self.copy(q, g.me, 2, g.left).start()
-        self.copy(q, g.me, 0, g.partner).start()
+        self.copy(q, g.me, 0, g.right).start()
+        either(
+            q, self.pair_last,
+            lambda q: self.copy(q, g.me, 1, g.left).start(),
+            lambda q: self.copy(q, g.me, 3, g.left).start(),
+        )
+        either(
+            q, self.pair_last,
+            lambda q: self.copy(q, g.me, 3, g.partner).start(),
+            lambda q: self.copy(q, g.me, 1, g.partner).start(),
+        )
 
     def pass_left(self, q):
         g = self.group
-        self.copy(q, g.left, 1, g.right).wait_recv()
-        self.copy(q, g.left, 5, g.right).start()
-
-    def pass_partner(self, q):
+        self.copy(q, g.left, 0, g.right).wait_recv()
+
+        def special(q):
+            self.copy(q, g.left, 2, g.right, 0, self.sub // 2).start()
+            self.copy(q, g.left, 3, g.partner).start()
+
+        either(q, self.pair_last, special, lambda q: self.copy(q, g.left, 3, g.right).start())
+
+    def pass_other(self, q):
         g = self.group
-        self.copy(q, g.partner, 0, g.partner).wait_recv()
-        self.copy(q, g.partner, 4, g.left).start()
-        self.copy(q, g.partner, 3, g.right).start()
-
-    def pass_corner(self, q):
+
+        def special(q):
+            self.copy(q, g.right, 1, g.left).wait_recv()
+            self.copy(q, g.right, 2, g.left, self.sub // 2, self.sub // 2).start()
+            self.copy(q, g.right, 3, g.partner).start()
+
+        def usual(q):
+            self.copy(q, g.partner, 1, g.partner).wait_recv()
+            self.copy(q, g.partner, 2, g.left).start()
+            self.copy(q, g.partner, 3, g.right).start()
+
+        either(q, self.pair_last, special, usual)
+
+    def pass_far(self, q):
         g = self.group
-        self.copy(q, g.at(1, 1 - g.half), 4, g.right).wait_recv()
-        self.copy(q, g.at(1, 1 - g.half), 6, g.left).start()
+
+        def special(q):
+            self.copy(q, g.at(2, g.half), 2, g.right).wait_recv()
+            self.copy(q, g.at(2, g.half), 3, g.partner).start()
+
+        def usual(q):
+            self.copy(q, g.at(1, 1 - g.half), 2, g.right).wait_recv()
+            self.copy(q, g.at(1, 1 - g.half), 3, g.left).start()
+
+        either(q, self.pair_last, special, usual)
 
     def last(self, q):
         rest = self.buf.at[q, pl.ds(0, 4 * self.sub), :]
@@ -71,67 +122,126 @@
 
 
 class Scatter:
-    def __init__(self, group, sums, place, out1, in1, out2, in2, out3, in3, keep, send, recv, sub):
+    def __init__(self, group, sums, place, out1, in1, out2, in2, out3, in3, out4, in4, keep, send, recv, sub, pair_first=()):
         self.group, self.sums, self.place = group, sums, place
         self.out1, self.in1, self.out2, self.in2 = out1, in1, out2, in2
-        self.out3, self.in3, self.keep = out3, in3, keep
-        self.send, self.recv, self.sub = send, recv, sub
+        self.out3, self.in3, self.out4, self.in4, self.keep = out3, in3, out4, in4, keep
+        self.send, self.recv, self.sub, self.pair_first = send, recv, sub, pair_first
 
     def rows(self, q, owner):
         start = pl.multiple_of(self.place(q, owner) * self.sub, self.sub)
-        return self.sums[q % SLOTS, pl.ds(start, self.sub), :]
-
-    def copy(self, q, message):
-        g = self.group
-        src, dst = {
-            0: (self.out1.at[q, 0], self.in1.at[q, 0]),
-            1: (self.out1.at[q, 1], self.in1.at[q, 1]),
-            2: (self.out2.at[q, 0], self.in2.at[q, 0]),
-            3: (self.out2.at[q, 1], self.in2.at[q, 1]),
-            4: (self.out3.at[q], self.in3.at[q]),
-        }[message]
-        to = g.partner if message == 4 else (g.right, g.left)[message % 2]
+        return (q % SLOTS, pl.ds(start, self.sub), slice(None))
+
+    def copy(self, q, src, dst, sem, to):
         return pltpu.make_async_remote_copy(
-            src, dst, self.send.at[0], self.recv.at[q, (0, 1, 2, 2, 3)[message]], device_id={g.axis: to}
-        )
+            src, dst, self.send.at[0], self.recv.at[q, sem], device_id={self.group.axis: to}
+        )
+
+    def side(self, q, side):
+        to = (self.group.right, self.group.left)[side]
+        return self.copy(q, self.out1.at[q, side], self.in1.at[q, side], side, to)
+
+    def near(self, q, side):
+        to = (self.group.right, self.group.left)[side]
+        rows = pl.ds(0, self.sub // 2)
+        return self.copy(q, self.out1.at[q, side, rows, :], self.in1.at[q, side, rows, :], side, to)
+
+    def double(self, q):
+        return self.copy(q, self.out2.at[q], self.in2.at[q], 2, self.group.partner)
+
+    def single(self, q):
+        return self.copy(q, self.out3.at[q], self.in3.at[q], 3, self.group.partner)
 
     def first(self, q):
-        for h in (0, 1):
-            self.out1[q, h] = self.rows(q, self.group.at(2, h)).astype(BF16)
-            self.copy(q, h).start()
+        g, sub = self.group, self.sub
+
+        def special(q):
+            for step in range(RING):
+                at = slice((step % 2) * sub, (step % 2 + 1) * sub)
+                self.out2[q, step // 2, at, :] = self.sums[self.rows(q, g.at(step, 1 - g.half))].astype(BF16)
+            self.double(q).start()
+
+        def usual(q):
+            for h in (0, 1):
+                self.out1[q, h] = self.sums[self.rows(q, g.at(2, h))].astype(BF16)
+                self.side(q, h).start()
+
+        either(q, self.pair_first, special, usual)
 
     def second(self, q):
         g, sub = self.group, self.sub
-        for side, step in ((0, 1), (1, 3)):
-            self.copy(q, side).wait_recv()
-            for h in (0, 1):
-                value = self.rows(q, g.at(step, h))
-                if h == side:
-                    value = value + self.in1[q, side].astype(F32)
-                self.out2[q, side, h * sub:(h + 1) * sub, :] = value.astype(BF16)
-            self.copy(q, 2 + side).start()
+
+        def special(q):
+            self.double(q).wait_recv()
+            for step in (2, 1, 3, 0):
+                at = slice((step % 2) * sub, (step % 2 + 1) * sub)
+                value = self.sums[self.rows(q, g.at(step, g.half))] + self.in2[q, step // 2, at, :].astype(F32)
+                if step == 2:
+                    for side in (0, 1):
+                        part = slice(side * sub // 2, (side + 1) * sub // 2)
+                        self.out1[q, side, 0:sub // 2, :] = value[part].astype(BF16)
+                        self.near(q, side).start()
+                elif step == 0:
+                    self.keep[q] = value
+                else:
+                    self.sums[self.rows(q, g.at(step, g.half))] = value
+
+        def usual(q):
+            for side, step in ((0, 1), (1, 3)):
+                self.side(q, side).wait_recv()
+                for h in (0, 1):
+                    value = self.sums[self.rows(q, g.at(step, h))]
+                    if h == side:
+                        value = value + self.in1[q, side].astype(F32)
+                    self.out2[q, side, h * sub:(h + 1) * sub, :] = value.astype(BF16)
+                to = (g.right, g.left)[side]
+                self.copy(q, self.out2.at[q, side], self.in2.at[q, side], 2, to).start()
+
+        either(q, self.pair_first, special, usual)
 
     def third(self, q):
         g, sub = self.group, self.sub
-        pltpu.make_async_remote_copy(
-            self.out2.at[q], self.in2.at[q], self.send.at[0], self.recv.at[q, 2], device_id={g.axis: g.right}
-        ).wait_recv()
-
-        def total(h):
-            rows = pl.ds(pl.multiple_of(h * sub, sub), sub)
-            return (
-                self.rows(q, g.at(0, h))
-                + self.in2[q, 0, rows, :].astype(F32)
-                + self.in2[q, 1, rows, :].astype(F32)
-            )
-
-        self.out3[q] = total(1 - g.half).astype(self.out3.dtype)
-        self.copy(q, 4).start()
-        self.keep[q] = total(g.half)
+
+        def special(q):
+            for side, step in ((0, 1), (1, 3)):
+                self.near(q, side).wait_recv()
+                value = self.sums[self.rows(q, g.at(step, g.half))]
+                part = slice(side * sub // 2, (side + 1) * sub // 2)
+                rest = slice((1 - side) * sub // 2, (2 - side) * sub // 2)
+                relayed = value[part] + self.in1[q, side, 0:sub // 2, :].astype(F32)
+                self.out4[q, side, part, :] = relayed.astype(BF16)
+                self.out4[q, side, rest, :] = value[rest].astype(BF16)
+                to = (g.right, g.left)[side]
+                self.copy(q, self.out4.at[q, side], self.in4.at[q, side], 3, to).start()
+
+        def usual(q):
+            self.copy(q, self.out2.at[q], self.in2.at[q], 2, g.right).wait_recv()
+
+            def total(h):
+                rows = pl.ds(pl.multiple_of(h * sub, sub), sub)
+                return (
+                    self.sums[self.rows(q, g.at(0, h))]
+                    + self.in2[q, 0, rows, :].astype(F32)
+                    + self.in2[q, 1, rows, :].astype(F32)
+                )
+
+            self.out3[q] = total(1 - g.half).astype(BF16)
+            self.single(q).start()
+            self.keep[q] = total(g.half)
+
+        either(q, self.pair_first, special, usual)
 
     def last(self, q):
-        self.copy(q, 4).wait_recv()
-        return self.keep[q] + self.in3[q].astype(F32)
+        def special(q):
+            self.copy(q, self.out4.at[q], self.in4.at[q], 3, self.group.right).wait_recv()
+            self.keep[q] += self.in4[q, 0].astype(F32) + self.in4[q, 1].astype(F32)
+
+        def usual(q):
+            self.single(q).wait_recv()
+            self.keep[q] += self.in3[q].astype(F32)
+
+        either(q, self.pair_first, special, usual)
+        return self.keep[q]
 
 
 def product(a, a_other, w, w_other, sums, q, arrived):
@@ -150,8 +260,8 @@
     res, encw, decw, encb, decb, active,
     codes_out, rebuilt_out,
     x_own, x_sib, c_own, c_sib, we_own, we_sib, wd_own, wd_sib, mask, made,
-    e_sums, e_out1, e_in1, e_out2, e_in2, e_out3, e_in3, e_keep,
-    d_sums, d_out1, d_in1, d_out2, d_in2, d_out3, d_in3, d_keep,
+    e_sums, e_out1, e_in1, e_out2, e_in2, e_out3, e_in3, e_out4, e_in4, e_keep,
+    d_sums, d_out1, d_in1, d_out2, d_in2, d_out3, d_in3, d_out4, d_in4, d_keep,
     a2a_send, a2a_recv, local_sem, wx_sem,
     xg_send, xg_recv, cg_send, cg_recv,
     xs_send, xs_recv, cs_send, cs_recv,
@@ -233,14 +343,14 @@
     swap.start()
 
     xg = Gather(lat, x_own, xg_send, xg_recv, sub)
-    cg = Gather(tok, c_own, cg_send, cg_recv, sub)
+    cg = Gather(tok, c_own, cg_send, cg_recv, sub, PAIR_LAST)
     er = Scatter(
         tok, e_sums, lambda q, owner: (owner - q + PARTS) % PARTS,
-        e_out1, e_in1, e_out2, e_in2, e_out3, e_in3, e_keep, er_send, er_recv, sub,
+        e_out1, e_in1, e_out2, e_in2, e_out3, e_in3, e_out4, e_in4, e_keep, er_send, er_recv, sub, PAIR_FIRST,
     )
     dr = Scatter(
         lat, d_sums, lambda q, owner: owner,
-        d_out1, d_in1, d_out2, d_in2, d_out3, d_in3, d_keep, dr_send, dr_recv, sub,
+        d_out1, d_in1, d_out2, d_in2, d_out3, d_in3, d_out4, d_in4, d_keep, dr_send, dr_recv, sub, LAT_FIRST,
     )
 
     def x_swap(q):
@@ -312,23 +422,23 @@
         rebuilt_copy(q).start()
 
     steps = [
-        (encode, 5),
-        (dr.third, 17),
-        (dr.second, 13),
-        (cg.pass_corner, 10),
-        (cg.pass_partner, 9),
+        (c_last, 12),
+        (dr.second, 14),
+        (cg.pass_left, 10),
+        (decode, 12),
         (er.second, 6),
-        (x_last, 4),
-        (xg.pass_corner, 3),
+        (er.third, 7),
+        (cg.pass_other, 9),
+        (cg.pass_far, 10),
+        (activate, 8),
+        (encode, 4),
         (xg.pass_left, 2),
+        (xg.pass_other, 1),
+        (finish, 17),
+        (xg.pass_far, 2),
         (x_first, 0),
-        (xg.pass_partner, 1),
-        (activate, 8),
-        (er.third, 7),
-        (decode, 11),
-        (finish, 19),
-        (cg.pass_left, 9),
-        (c_last, 10),
+        (dr.third, 15),
+        (x_last, 3),
     ]
     rounds = PARTS + max(lag for _, lag in steps)
 
@@ -383,6 +493,8 @@
             pltpu.VMEM((PARTS, 2, 2 * sub, width), BF16),
             pltpu.VMEM((PARTS, sub, width), BF16),
             pltpu.VMEM((PARTS, sub, width), BF16),
+            pltpu.VMEM((PARTS, 2, sub, width), BF16),
+            pltpu.VMEM((PARTS, 2, sub, width), BF16),
             pltpu.VMEM((PARTS, sub, width), F32),
         ]
 

time: 128 us -> 122 us (0.953)
  Pallas kernels: 126 us -> 121 us
    pallas_call x1, Pallas kernels: 124 us -> 119 us  [per_device(): pl.pallas_call(kernel, out_shape=(jax.ShapeDtypeStruct((rows, latents), B...]
where the time goes in v3:
time: 122 us
  Pallas kernels  121 us (99%)
    pallas_call x1, Pallas kernels, per_device(): pl.pallas_call(kernel, out_shape=(jax.ShapeDtypeStruct((rows, latents), B...  119 us

profile of v3, /device:TPU:0, one launch (start us, length us, event | category | flops | bytes accessed | tf_op | source)
XLA Modules:
  0.0 121.9 jit_solution(9942487167433154333)
XLA Ops:
  0.6 119.0 %shard_map.77 = (bf16[256,2048]{1,0:T(8,128)(2,1)}, bf16[256,1024]{1,0:T(8,128)(2,1)}) custom-call(bf16[256,1024]{1,0:T(8,128)(2,1)} %bitcast.7, bf16[1024,2048]{1,0:T(8,128)(2,1)} %bitcast.5, bf16[2048,1024]{1,0:T(8,128)(2,1)} %bitcast.6, f32[1,2048]{1,0:T(1,128)} %bitcast.8, f32[1,1024]{1,0:T(1,128)} %decb.1, s32[256,2048]{1,0:T(8,128)} %active.1), custom_call_target="tpu_custom_call" | custom-call | tf_op jit(solution)/shard_map/pallas_call | solution.py:503
  119.6 2.3 %shard_map.78 = (bf16[256,2048]{1,0:T(8,128)(2,1)}, bf16[256,1024]{1,0:T(8,128)(2,1)}) custom-call(bf16[256,2048]{1,0:T(8,128)(2,1)} %get-tuple-element.6.codes_in, bf16[256,1024]{1,0:T(8,128)(2,1)} %get-tuple-element.7.rebuilt_in), custom_call_target="tpu_custom_call" | custom-call | tf_op jit(solution)/shard_map/pallas_call | solution.py:528

commit v4 on v3

--- a/solution.py
+++ b/solution.py
@@ -7,7 +7,7 @@
 
 PARTS = 8
 SLOTS = 6
-PAIR_FIRST = (5, 6, 7)
+PAIR_FIRST = (5, 7)
 LAT_FIRST = ()
 PAIR_LAST = ()
 RING = 4

time: 122 us -> 122 us (level)
  no operation moved by 1% of the time
where the time goes in v4:
time: 122 us
  Pallas kernels  121 us (99%)
    pallas_call x1, Pallas kernels, per_device(): pl.pallas_call(kernel, out_shape=(jax.ShapeDtypeStruct((rows, latents), B...  119 us

profile of v4, /device:TPU:0, one launch (start us, length us, event | category | flops | bytes accessed | tf_op | source)
XLA Modules:
  0.0 121.9 jit_solution(8470309766713677346)
XLA Ops:
  0.6 119.0 %shard_map.77 = (bf16[256,2048]{1,0:T(8,128)(2,1)}, bf16[256,1024]{1,0:T(8,128)(2,1)}) custom-call(bf16[256,1024]{1,0:T(8,128)(2,1)} %bitcast.7, bf16[1024,2048]{1,0:T(8,128)(2,1)} %bitcast.5, bf16[2048,1024]{1,0:T(8,128)(2,1)} %bitcast.6, f32[1,2048]{1,0:T(1,128)} %bitcast.8, f32[1,1024]{1,0:T(1,128)} %decb.1, s32[256,2048]{1,0:T(8,128)} %active.1), custom_call_target="tpu_custom_call" | custom-call | tf_op jit(solution)/shard_map/pallas_call | solution.py:503
  119.6 2.3 %shard_map.78 = (bf16[256,2048]{1,0:T(8,128)(2,1)}, bf16[256,1024]{1,0:T(8,128)(2,1)}) custom-call(bf16[256,2048]{1,0:T(8,128)(2,1)} %get-tuple-element.6.codes_in, bf16[256,1024]{1,0:T(8,128)(2,1)} %get-tuple-element.7.rebuilt_in), custom_call_target="tpu_custom_call" | custom-call | tf_op jit(solution)/shard_map/pallas_call | solution.py:528
